TPU v7x, 512 devices: a whole 4x4x16 slice. The times are simulated.
512 devices in a mesh: req: 32 (over y, z_lo), head: 16 (over x, z_hi, core).
Axes of the slice: x: 4, y: 4, z: 16 (z_hi: 2, z_lo: 8; z = z_hi * 8 + z_lo), core: 2. Of those that a mesh axis runs over, the one named last changes fastest.
Arguments:
- hidden: bfloat16 [256, 2048], P('req', 'head'), may hold values from -6 to 6
- attn_gain: float32 [2048], replicated, may hold values from 0.1 to 1.9
- q_weight: bfloat16 [2048, 2048], P(None, 'head'), may hold values from -0.125 to 0.125
- gate_weight: bfloat16 [2048, 2048], P(None, 'head'), may hold values from -0.125 to 0.125
- key_value_weight: bfloat16 [2048, 2048], P(None, 'head'), may hold values from -0.125 to 0.125
- q_gain: float32 [128], replicated, may hold values from 0.5 to 1.5
- k_gain: float32 [128], replicated, may hold values from 0.5 to 2
- out_weight: bfloat16 [2048, 2048], P('head'), may hold values from -0.5 to 0.5
- prompt_key_cache: bfloat16 [32, 4096, 8, 128], P('req', 'head'), may hold values from -3.5 to 3.5
- prompt_value_cache: bfloat16 [32, 4096, 8, 128], P('req', 'head'), may hold values from -6 to 6
- tail_key_cache: bfloat16 [32, 4, 256, 8, 128], P('req', None, 'head'), may hold values from -3.5 to 3.5
- tail_value_cache: bfloat16 [32, 4, 256, 8, 128], P('req', None, 'head'), may hold values from -6 to 6
- mlp_gain: float32 [2048], replicated, may hold values from 0.1 to 1.9
- mlp_gate: bfloat16 [2048, 6144], P('req', 'head'), may hold values from -0.125 to 0.125
- mlp_up: bfloat16 [2048, 6144], P('req', 'head'), may hold values from -0.125 to 0.125
- mlp_down: bfloat16 [6144, 2048], P('head'), may hold values from -0.109375 to 0.109375
- final_gain: float32 [2048], P('head'), may hold values from 0.1 to 1.9
- score_weight: float32 [2048], P('head'), may hold values from -0.125 to 0.125
- prompt_lengths: int32 [32], replicated, may hold values from 1 to 4096, 65536 in all
- tail_lengths: int32 [32, 4], replicated, may hold values from 1 to 256, 512 in all within a row
- group_prompt: int32 [32], replicated, may hold values from 0 to 31, each once
Outputs:
- new_hidden: bfloat16 [256, 2048], P('req', 'head')
- score: float32 [256], P('req')
Inputs may be any that keep to these rules, and one draw needn't show every extreme that they name: `group_prompt`: every prompt is held by exactly one group. `prompt_lengths`: one prompt has exactly 4096 prefix tokens. `tail_lengths`: in every prompt one continuation has exactly 256 tail tokens.
All inputs are finite; a program needn't handle non-finite values.
Results may differ from a plain program's by a relative error of at most 0.023.
Values may be sent and summed in bfloat16 or wider, within the bound.
A program may use at most 64 MiB of HBM per device.

v0:
```python
import math
import jax
import jax.numpy as jnp
from jax import lax
from jax.sharding import PartitionSpec as P

EPS = 1e-06
THETA = 1000000.0


def rms_scale(value, gain):
    return value * lax.rsqrt(jnp.mean(value * value, axis=-1, keepdims=True) + EPS) * gain


def rotate(value, position):
    head_width = value.shape[-1]
    half_width = head_width // 2
    frequency = jnp.exp(
        -math.log(THETA) * 2.0 * jnp.arange(half_width, dtype=jnp.float32) / head_width
    )
    angles = position.astype(jnp.float32)[:, None] * frequency[None, :]
    cosine = jnp.cos(angles)[:, None, :]
    sine_part = jnp.sin(angles)[:, None, :]
    first_half = value[..., :half_width]
    second_half = value[..., half_width:]
    return jnp.concatenate(
        [
            first_half * cosine - second_half * sine_part,
            second_half * cosine + first_half * sine_part,
        ],
        axis=-1,
    )


def shards(
    hidden,
    attn_gain,
    q_weight,
    gate_weight,
    key_value_weight,
    q_gain,
    k_gain,
    out_weight,
    prompt_key_cache,
    prompt_value_cache,
    tail_key_cache,
    tail_value_cache,
    mlp_gain,
    mlp_gate,
    mlp_up,
    mlp_down,
    final_gain,
    score_weight,
    prompt_lengths,
    tail_lengths,
    group_prompt,
):
    head_count = lax.axis_size("head")
    group_count = lax.axis_size("req")
    group_id = lax.axis_index("req")
    head_place = lax.axis_index("head")
    count_of_rows = hidden.shape[0]
    model_width = attn_gain.shape[0]
    head_width = q_gain.shape[0]
    own_heads = q_weight.shape[1] // head_width
    all_heads = own_heads * head_count
    block_count = key_value_weight.shape[1] // head_width
    kv_heads = block_count * head_count // 2
    sharing_count = all_heads // kv_heads
    cont_count = tail_lengths.shape[1]
    new_count = count_of_rows // cont_count
    score_scale = 1.0 / math.sqrt(head_width)
    slot_ids = jnp.arange(group_count, dtype=jnp.int32)
    prompt_id = jnp.sum(jnp.where(slot_ids == group_id, group_prompt, 0))
    prompt_len = jnp.sum(jnp.where(slot_ids == prompt_id, prompt_lengths, 0))
    tail_row = jnp.sum(jnp.where((slot_ids == prompt_id)[:, None], tail_lengths, 0), axis=0)
    owner_group = jnp.sum(
        jnp.where(group_prompt[None, :] == slot_ids[:, None], slot_ids[None, :], 0), axis=1
    )
    position = (
        prompt_len + tail_row[:, None] + jnp.arange(new_count, dtype=jnp.int32)[None, :]
    ).reshape(count_of_rows)
    whole_rows = lax.all_gather(hidden, "head", axis=1, tiled=True)
    block_rows = whole_rows.astype(jnp.float32)
    normalized_hidden = rms_scale(block_rows, attn_gain).astype(jnp.bfloat16)
    gate_pre = jnp.dot(normalized_hidden, gate_weight, preferred_element_type=jnp.float32)
    query_rows = jnp.dot(normalized_hidden, q_weight, preferred_element_type=jnp.float32).reshape(
        count_of_rows, own_heads, head_width
    )
    query_rows = rotate(rms_scale(query_rows, q_gain), position).astype(jnp.bfloat16)
    projected_rows = jnp.dot(
        normalized_hidden, key_value_weight, preferred_element_type=jnp.float32
    ).reshape(count_of_rows, block_count, head_width)
    is_key = (head_place * block_count + jnp.arange(block_count, dtype=jnp.int32)) % 2 == 0
    keyed = rotate(rms_scale(projected_rows, k_gain), position)
    fresh = jnp.where(is_key[None, :, None], keyed, projected_rows).astype(jnp.bfloat16)
    all_queries, all_fresh = (
        lax.all_gather(
            query_rows.reshape(count_of_rows, own_heads * head_width), "head", axis=1, tiled=True
        ),
        lax.all_gather(
            fresh.reshape(count_of_rows, block_count * head_width), "head", axis=1, tiled=True
        ),
    )
    query_groups = all_queries.reshape(count_of_rows, kv_heads, sharing_count, head_width)
    local_keys = prompt_key_cache[0]
    local_values = prompt_value_cache[0]
    span_length = local_keys.shape[0]
    block_size = min(128, span_length)
    block_total = span_length // block_size
    span_start = head_place * span_length

    def prefix_block(block_id, sums):
        numer_acc, total_acc = sums
        key_block = lax.dynamic_slice_in_dim(local_keys, block_id * block_size, block_size, 0)
        value_block = lax.dynamic_slice_in_dim(local_values, block_id * block_size, block_size, 0)
        scores = (
            jnp.einsum(
                "rkgd,tkd->rkgt", query_groups, key_block, preferred_element_type=jnp.float32
            )
            * score_scale
        )
        slot_pos = span_start + block_id * block_size + jnp.arange(block_size, dtype=jnp.int32)
        attention_weights = jnp.where(
            slot_pos[None, None, None, :] < prompt_len, jnp.exp(scores), 0.0
        )
        numer_acc = numer_acc + jnp.einsum(
            "rkgt,tkd->rkgd",
            attention_weights.astype(jnp.bfloat16),
            value_block,
            preferred_element_type=jnp.float32,
        )
        return (numer_acc, total_acc + jnp.sum(attention_weights, axis=-1))

    start_sums = (
        jnp.zeros((count_of_rows, kv_heads, sharing_count, head_width), jnp.float32),
        jnp.zeros((count_of_rows, kv_heads, sharing_count), jnp.float32),
    )
    numerator, denominator = lax.fori_loop(0, block_total, prefix_block, start_sums)
    continuation_rows = query_groups.reshape(
        cont_count, new_count, kv_heads, sharing_count, head_width
    )
    tkeys = tail_key_cache[0]
    tail_value_rows = tail_value_cache[0]
    tail_span = tkeys.shape[1]
    scores = (
        jnp.einsum(
            "cjkgd,ctkd->cjkgt", continuation_rows, tkeys, preferred_element_type=jnp.float32
        )
        * score_scale
    )
    tail_pos = head_place * tail_span + jnp.arange(tail_span, dtype=jnp.int32)
    tail_live = tail_pos[None, :] < tail_row[:, None]
    attention_weights = jnp.where(tail_live[:, None, None, None, :], jnp.exp(scores), 0.0)
    numerator = numerator + jnp.einsum(
        "ihbyw,iwbs->ihbys",
        attention_weights.astype(jnp.bfloat16),
        tail_value_rows,
        preferred_element_type=jnp.float32,
    ).reshape(count_of_rows, kv_heads, sharing_count, head_width)
    denominator = denominator + jnp.sum(attention_weights, axis=-1).reshape(
        count_of_rows, kv_heads, sharing_count
    )
    numerator = numerator.reshape(count_of_rows, all_heads, head_width)
    denominator = denominator.reshape(count_of_rows, all_heads)
    numer_sum, total_sum = lax.psum((numerator, denominator), "head")
    numer_own = lax.dynamic_slice_in_dim(numer_sum, head_place * own_heads, own_heads, 1)
    total_own = lax.dynamic_slice_in_dim(total_sum, head_place * own_heads, own_heads, 1)
    fresh_all = all_fresh.reshape(count_of_rows, kv_heads, 2, head_width)
    own_kv = max(own_heads // sharing_count, 1)
    per_kv = own_heads // own_kv
    nearby = lax.dynamic_slice_in_dim(fresh_all, head_place * own_heads // sharing_count, own_kv, 1)
    own_queries = query_rows.reshape(cont_count, new_count, own_kv, per_kv, head_width)
    recent_key_rows = nearby[:, :, 0].reshape(cont_count, new_count, own_kv, head_width)
    recent_value_rows = nearby[:, :, 1].reshape(cont_count, new_count, own_kv, head_width)
    scores = (
        jnp.einsum(
            "cjkgd,cukd->cjkgu", own_queries, recent_key_rows, preferred_element_type=jnp.float32
        )
        * score_scale
    )
    causal = (
        jnp.arange(new_count, dtype=jnp.int32)[None, :]
        <= jnp.arange(new_count, dtype=jnp.int32)[:, None]
    )
    attention_weights = jnp.where(causal[None, :, None, None, :], jnp.exp(scores), 0.0)
    numer_own = numer_own + jnp.einsum(
        "bfmne,beml->bfmnl",
        attention_weights.astype(jnp.bfloat16),
        recent_value_rows,
        preferred_element_type=jnp.float32,
    ).reshape(count_of_rows, own_heads, head_width)
    total_own = total_own + jnp.sum(attention_weights, axis=-1).reshape(count_of_rows, own_heads)
    attention = (numer_own / total_own[..., None]).reshape(count_of_rows, own_heads * head_width)
    gated = (attention * jax.nn.sigmoid(gate_pre)).astype(jnp.bfloat16)
    mixed = lax.psum(jnp.dot(gated, out_weight, preferred_element_type=jnp.float32), "head")
    attended = (block_rows + mixed).astype(jnp.bfloat16)
    col_width = model_width // head_count
    wide_rows = attended.astype(jnp.float32)
    mlp_in = rms_scale(wide_rows, mlp_gain).astype(jnp.bfloat16)
    column_in = lax.all_to_all(mlp_in, "req", split_axis=1, concat_axis=0, tiled=True)
    gate_part = jnp.dot(column_in, mlp_gate, preferred_element_type=jnp.float32)
    up_part = jnp.dot(column_in, mlp_up, preferred_element_type=jnp.float32)
    gate_own, up_own = (
        lax.psum_scatter(gate_part, "req", scatter_dimension=0, tiled=True),
        lax.psum_scatter(up_part, "req", scatter_dimension=0, tiled=True),
    )
    act_rows = (jax.nn.silu(gate_own) * up_own).astype(jnp.bfloat16)
    down_part = jnp.dot(act_rows, mlp_down, preferred_element_type=jnp.float32)
    down_total = lax.psum(down_part, "head")
    added = lax.dynamic_slice_in_dim(down_total, head_place * col_width, col_width, 1)
    residual = lax.dynamic_slice_in_dim(wide_rows, head_place * col_width, col_width, 1)
    finished = (residual + added).astype(jnp.bfloat16)
    everyone = lax.all_gather(finished, "req", axis=0, tiled=True)
    my_owner = jnp.sum(jnp.where(slot_ids == group_id, owner_group, 0))
    new_hidden = lax.dynamic_slice_in_dim(everyone, my_owner * count_of_rows, count_of_rows, 0)
    final_rows = new_hidden.astype(jnp.float32)
    squares, product = lax.psum(
        (
            jnp.sum(final_rows * final_rows, axis=-1),
            jnp.sum(final_rows * final_gain * score_weight, axis=-1),
        ),
        "head",
    )
    score = product * lax.rsqrt(squares / model_width + EPS)
    return (new_hidden, score)


def solution(mesh):
    return jax.shard_map(
        shards,
        mesh=mesh,
        in_specs=(
            P("req", "head"),
            P(),
            P(None, "head"),
            P(None, "head"),
            P(None, "head"),
            P(),
            P(),
            P("head", None),
            P("req", "head", None, None),
            P("req", "head", None, None),
            P("req", None, "head", None, None),
            P("req", None, "head", None, None),
            P(),
            P("req", "head"),
            P("req", "head"),
            P("head", None),
            P("head"),
            P("head"),
            P(),
            P(),
            P(),
        ),
        out_specs=(P("req", "head"), P("req")),
        check_vma=False,
    )
```

profile of v0, /device:TPU:1, one launch (start us, length us, event | category | flops | bytes accessed | tf_op | source)
XLA Modules:
  0.0 1502.3 jit_solution(17086110039047880849)
XLA Ops:
  7.3 51.2 %all_gather.12 = bf16[8,2048]{1,0:T(8,128)(2,1)S(1)} all-gather(bf16[8,128]{1,0:T(8,128)(2,1)} %param.23), channel_id=1, replica_groups=mesh['req'=32,'head'=16] {'head'}, dimensions={1}, use_global_device_ids=true | all-gather | bytes 34816 | tf_op jit(solution)/shard_map/all_gather | solution.py:83
  59.3 1.3 fusion.70
  61.3 2.0 select_reduce_fusion.2
  63.3 0.8 select_reduce_fusion.1
  65.0 1.4 multiply_reduce_fusion.2
  67.3 33.8 %all_gather.13 = bf16[8,2048]{1,0:T(8,128)(2,1)S(1)} all-gather(bf16[8,128]{1,0:T(8,128)(2,1)S(1)} %pad_maximum_fusion), channel_id=1, replica_groups=mesh['req'=32,'head'=16] {'head'}, dimensions={1}, use_global_device_ids=true | all-gather | bytes 34816 | tf_op jit(solution)/shard_map/all_gather | solution.py:98
  101.1 1.4 copy_bitcast_fusion
  102.6 2.6 while.16
  105.6 1.1 convolution_bitcast_fusion.1
  108.2 43.8 %all_gather.14 = bf16[8,2048]{1,0:T(8,128)(2,1)S(1)} all-gather(bf16[8,128]{1,0:T(8,128)(2,1)S(1)} %fusion.57), channel_id=1, replica_groups=mesh['req'=32,'head'=16] {'head'}, dimensions={1}, use_global_device_ids=true | all-gather | bytes 34816 | tf_op jit(solution)/shard_map/all_gather | solution.py:101
  153.0 62.0 %psum.43 = f32[8,16]{0,1:T(8,128)S(1)} all-reduce(f32[8,16]{0,1:T(8,128)S(1)} %bitcast.127), channel_id=1, replica_groups=mesh['req'=32,'head'=16] {'head'}, use_global_device_ids=true, to_apply=%region_11.12 | all-reduce | flops 128 | bytes 1024 | tf_op jit(solution)/shard_map/psum | solution.py:166
  215.2 132.7 %all-reduce.9.cloned.1.call-done = f32[8,16,128]{2,0,1:T(8,128)} async-done(((f32[8,16,128]{2,0,1:T(8,128)}), f32[8,16,128]{2,0,1:T(8,128)}) %all-reduce.9.cloned.1.call-update) | async-done | bytes 65552 | tf_op jit(solution)/shard_map/psum | solution.py:166
  347.9 1.7 fusion.20
  349.7 242.6 %all-reduce.11.cloned.1.call-done = f32[8,2048]{1,0:T(8,128)} async-done(((f32[8,2048]{1,0:T(8,128)}), f32[8,2048]{1,0:T(8,128)}) %all-reduce.11.cloned.1.call-update) | async-done | bytes 65552 | tf_op jit(solution)/shard_map/psum | solution.py:196
  592.3 1.0 multiply_reduce_fusion
  593.7 16.2 %all_to_all.19 = bf16[32,2,256]{2,1,0:T(2,128)(2,1)S(1)} all-to-all(bf16[32,2,256]{2,1,0:T(2,128)(2,1)S(1)} %reshape.325), channel_id=1, replica_groups=mesh['req'=32,'head'=16] {'req'}, dimensions={0} | all-to-all | bytes 65536 | tf_op jit(solution)/shard_map/all_to_all | solution.py:201
  610.1 0.9 fusion.27
  611.0 1.0 fusion.29
  612.0 1.3 dynamic-slice
  613.9 428.9 %all-reduce.15.cloned.1.call-done = (f32[256,384]{1,0:T(8,128)}, f32[256,384]{1,0:T(8,128)}) async-done(((f32[256,384]{1,0:T(8,128)}, f32[256,384]{1,0:T(8,128)}), (f32[256,384]{1,0:T(8,128)}, f32[256,384]{1,0:T(8,128)})) %all-reduce.15.cloned.1.call-update) | async-done | bytes 786448
  1042.8 1.7 fusion.35
  1045.2 263.3 %all-reduce.13.cloned.1.call-done = f32[8,2048]{1,0:T(8,128)} async-done(((f32[8,2048]{1,0:T(8,128)}), f32[8,2048]{1,0:T(8,128)}) %all-reduce.13.cloned.1.call-update) | async-done | bytes 65552 | tf_op jit(solution)/shard_map/psum | solution.py:210
  1309.2 101.1 %all_gather.15 = bf16[256,128]{1,0:T(8,128)(2,1)S(1)} all-gather(bf16[8,128]{1,0:T(8,128)(2,1)S(1)} %add_convert_fusion), channel_id=1, replica_groups=mesh['req'=32,'head'=16] {'req'}, dimensions={0}, use_global_device_ids=true | all-gather | bytes 67584 | tf_op jit(solution)/shard_map/all_gather | solution.py:214
  1411.0 84.3 %all-reduce.3 = (f32[8]{0:T(128)S(1)}, f32[8]{0:T(128)S(1)}) all-reduce(f32[8]{0:T(128)S(1)} %get-tuple-element.172, f32[8]{0:T(128)S(1)} %get-tuple-element.171), channel_id=1, replica_groups=mesh['req'=32,'head'=16] {'head'}, use_global_device_ids=true, to_apply=%region_21.22 | all-reduce | flops 16 | bytes 128 | tf_op jit(solution)/shard_map/psum | solution.py:218
  (90 shorter events, 11.5 us)
Async XLA Ops:
  7.2 1035.7 %copy-start = (bf16[384,2048]{1,0:T(8,128)(2,1)S(1)}, bf16[384,2048]{1,0:T(8,128)(2,1)}, u32[]{:S(2)}) copy-start(bf16[384,2048]{1,0:T(8,128)(2,1)} %param.38) | copy-start | bytes 4718596
  7.2 340.7 %all-reduce.9.cloned.1.call-start = ((), (), s32[]{:S(2)}) async-start(), calls=%async_computation.1 | async-start | bytes 131072 | tf_op jit(solution)/shard_map/psum | solution.py:166
  102.5 2.8 copy-start.11
  102.5 5.0 copy-start.3
  102.5 5.0 copy-start.4
  105.2 2.8 copy-start.8
  105.2 242.7 %copy-start.1 = (bf16[128,2048]{1,0:T(8,128)(2,1)S(1)}, bf16[128,2048]{1,0:T(8,128)(2,1)}, u32[]{:S(2)}) copy-start(bf16[128,2048]{1,0:T(8,128)(2,1)} %param.30) | copy-start | bytes 1572868
  105.2 242.7 %copy-start.2 = (bf16[2048,128]{1,0:T(8,128)(2,1)S(1)}, bf16[2048,128]{1,0:T(8,128)(2,1)}, u32[]{:S(2)}) copy-start(bf16[2048,128]{1,0:T(8,128)(2,1)} %param.26) | copy-start | bytes 1572868
  105.6 487.7 %copy-start.7 = (f32[2048]{0:T(1024)S(1)}, f32[2048]{0:T(1024)}, u32[]{:S(2)}) copy-start(f32[2048]{0:T(1024)} %param.35) | copy-start | bytes 24580
  106.8 503.3 %copy-start.5 = (bf16[64,384]{1,0:T(8,128)(2,1)S(1)}, bf16[64,384]{1,0:T(8,128)(2,1)}, u32[]{:S(2)}) copy-start(bf16[64,384]{1,0:T(8,128)(2,1)} %param.37) | copy-start | bytes 147460
  107.4 484.9 %all-reduce.11.cloned.1.call-start = ((), (), s32[]{:S(2)}) async-start(), calls=%async_computation.2 | async-start | bytes 131072 | tf_op jit(solution)/shard_map/psum | solution.py:196
  107.6 503.4 %copy-start.6 = (bf16[64,384]{1,0:T(8,128)(2,1)S(1)}, bf16[64,384]{1,0:T(8,128)(2,1)}, u32[]{:S(2)}) copy-start(bf16[64,384]{1,0:T(8,128)(2,1)} %param.36) | copy-start | bytes 147460
  349.7 693.2 %all-reduce.15.cloned.1.call-start = ((), (), s32[]{:S(2)}) async-start(), calls=%async_computation.4 | async-start | bytes 1572864
  611.0 799.3 %copy-start.9 = (f32[128]{0:T(128)S(1)}, f32[128]{0:T(128)}, u32[]{:S(2)}) copy-start(f32[128]{0:T(128)} %param.40) | copy-start | bytes 1540
  611.0 799.3 %copy-start.10 = (f32[128]{0:T(128)S(1)}, f32[128]{0:T(128)}, u32[]{:S(2)}) copy-start(f32[128]{0:T(128)} %param.39) | copy-start | bytes 1540
  612.0 696.5 %all-reduce.13.cloned.1.call-start = ((), (), s32[]{:S(2)}) async-start(), calls=%async_computation.3 | async-start | bytes 131072 | tf_op jit(solution)/shard_map/psum | solution.py:210
Sparse Core Ops, SparseCore 0:
  107.6 240.3 all-reduce.8
  351.1 241.2 all-reduce.10
  612.1 430.6 all-reduce.14
  1045.9 262.5 all-reduce.12
where the time goes:
time: 1500 us
  waiting for transfers between devices  1070 us (71%)
  blocking collectives  392 us (26%)
  between operations  15.4 us (1%)
    unnamed x5, waiting for transfers between devices  429 us
    psum x1, waiting for transfers between devices, shards(): down_total = lax.psum(down_part, 'head')  263 us
    psum x1, waiting for transfers between devices, shards(): lax.psum(jnp.dot(gated, out_weight, preferred_element_type=jnp.float32),...  243 us
    psum x1, waiting for transfers between devices, shards(): numer_sum, total_sum = lax.psum((numerator, denominator), 'head')  133 us
    all_gather x1, blocking collectives, shards(): everyone = lax.all_gather(finished, 'req', axis=0, tiled=True)  101 us
    psum x1, blocking collectives, shards(): lax.psum((jnp.sum(final_rows * final_rows, axis=-1), jnp.sum(final_rows *...  84.3 us
    psum x1, blocking collectives, shards(): numer_sum, total_sum = lax.psum((numerator, denominator), 'head')  62 us
    all_gather x1, blocking collectives, shards(): whole_rows = lax.all_gather(hidden, 'head', axis=1, tiled=True)  51.2 us
  transfers between devices with their start and end apart: 4, of which 4 were waited for; matrix products, arithmetic and copies ran while one was open for 0% of the time, Pallas kernels for 0%

commit v1 on v0

--- a/solution.py
+++ b/solution.py
@@ -95,8 +95,17 @@
     keyed = rotate(rms_scale(projected_rows, k_gain), position)
     fresh = jnp.where(is_key[None, :, None], keyed, projected_rows).astype(jnp.bfloat16)
     all_queries, all_fresh = (
-        lax.all_gather(
-            query_rows.reshape(count_of_rows, own_heads * head_width), "head", axis=1, tiled=True
+        jnp.concatenate(
+            lax.all_to_all(
+                jnp.stack(
+                    [query_rows.reshape(count_of_rows, own_heads * head_width)]
+                    * lax.axis_size("head")
+                ),
+                "head",
+                0,
+                0,
+            ),
+            axis=1,
         ),
         lax.all_gather(
             fresh.reshape(count_of_rows, block_count * head_width), "head", axis=1, tiled=True

time: 1500 us -> 1580 us (1.053)
  waiting for transfers between devices: 1070 us -> 1170 us
  blocking collectives: 392 us -> 361 us
    psum x1, waiting for transfers between devices: 133 us -> 235 us  [shards(): numer_sum, total_sum = lax.psum((numerator, denominator), 'head')]
    all_gather x1 -> x0, blocking collectives: 33.8 us -> none  [shards(): lax.all_gather(query_rows.reshape(count_of_rows, own_heads * head_width),...]
  transfers between devices with their start and end apart: 4 -> 5, of which waited for: 4 -> 4; matrix products, arithmetic and copies ran while one was open for 0% -> 0% of each run, Pallas kernels for 0% -> 0%
where the time goes in v1:
time: 1580 us
  waiting for transfers between devices  1170 us (74%)
  blocking collectives  361 us (23%)
    unnamed x5, waiting for transfers between devices  429 us
    psum x1, waiting for transfers between devices, shards(): down_total = lax.psum(down_part, 'head')  263 us
    psum x1, waiting for transfers between devices, shards(): lax.psum(jnp.dot(gated, out_weight, preferred_element_type=jnp.float32),...  243 us
    psum x1, waiting for transfers between devices, shards(): numer_sum, total_sum = lax.psum((numerator, denominator), 'head')  235 us
    all_gather x1, blocking collectives, shards(): everyone = lax.all_gather(finished, 'req', axis=0, tiled=True)  101 us
    psum x1, blocking collectives, shards(): lax.psum((jnp.sum(final_rows * final_rows, axis=-1), jnp.sum(final_rows *...  84.3 us
    psum x1, blocking collectives, shards(): numer_sum, total_sum = lax.psum((numerator, denominator), 'head')  62 us
    all_gather x1, blocking collectives, shards(): whole_rows = lax.all_gather(hidden, 'head', axis=1, tiled=True)  51.2 us
  transfers between devices with their start and end apart: 5, of which 4 were waited for; matrix products, arithmetic and copies ran while one was open for 0% of the time, Pallas kernels for 0%

profile of v1, /device:TPU:1, one launch (start us, length us, event | category | flops | bytes accessed | tf_op | source)
XLA Modules:
  0.0 1577.5 jit_solution(15030720127550050280)
XLA Ops:
  7.2 51.2 %all_gather.9 = bf16[8,2048]{1,0:T(8,128)(2,1)S(1)} all-gather(bf16[8,128]{1,0:T(8,128)(2,1)} %param.23), channel_id=1, replica_groups=mesh['req'=32,'head'=16] {'head'}, dimensions={1}, use_global_device_ids=true | all-gather | bytes 34816 | tf_op jit(solution)/shard_map/all_gather | solution.py:83
  59.3 1.3 fusion.70
  61.2 2.0 select_reduce_fusion.2
  63.2 0.8 select_reduce_fusion.1
  64.8 1.4 multiply_reduce_fusion.2
  67.8 3.5 all-to-all-start
  71.3 1.4 multiply_reduce_fusion.1
  73.7 46.2 %all_gather.10 = bf16[8,2048]{1,0:T(8,128)(2,1)S(1)} all-gather(bf16[8,128]{1,0:T(8,128)(2,1)S(1)} %fusion.57), channel_id=1, replica_groups=mesh['req'=32,'head'=16] {'head'}, dimensions={1}, use_global_device_ids=true | all-gather | bytes 34816 | tf_op jit(solution)/shard_map/all_gather | solution.py:110
  120.7 1.2 copy_bitcast_fusion
  122.2 2.5 while.16
  125.3 62.0 %psum.43 = f32[8,16]{0,1:T(8,128)S(1)} all-reduce(f32[8,16]{0,1:T(8,128)S(1)} %bitcast.132), channel_id=1, replica_groups=mesh['req'=32,'head'=16] {'head'}, use_global_device_ids=true, to_apply=%region_11.12 | all-reduce | flops 128 | bytes 1024 | tf_op jit(solution)/shard_map/psum | solution.py:175
  188.3 234.9 %all-reduce.9.cloned.1.call-done = f32[8,16,128]{2,0,1:T(8,128)} async-done(((f32[8,16,128]{2,0,1:T(8,128)}), f32[8,16,128]{2,0,1:T(8,128)}) %all-reduce.9.cloned.1.call-update) | async-done | bytes 65552 | tf_op jit(solution)/shard_map/psum | solution.py:175
  423.2 1.7 fusion.20
  425.0 242.6 %all-reduce.11.cloned.1.call-done = f32[8,2048]{1,0:T(8,128)} async-done(((f32[8,2048]{1,0:T(8,128)}), f32[8,2048]{1,0:T(8,128)}) %all-reduce.11.cloned.1.call-update) | async-done | bytes 65552 | tf_op jit(solution)/shard_map/psum | solution.py:205
  667.6 1.0 multiply_reduce_fusion
  668.9 16.2 %all_to_all.24 = bf16[32,2,256]{2,1,0:T(2,128)(2,1)S(1)} all-to-all(bf16[32,2,256]{2,1,0:T(2,128)(2,1)S(1)} %reshape.329), channel_id=1, replica_groups=mesh['req'=32,'head'=16] {'req'}, dimensions={0} | all-to-all | bytes 65536 | tf_op jit(solution)/shard_map/all_to_all | solution.py:210
  685.3 0.9 fusion.27
  686.3 1.0 fusion.29
  687.3 1.3 dynamic-slice
  689.2 428.8 %all-reduce.15.cloned.1.call-done = (f32[256,384]{1,0:T(8,128)}, f32[256,384]{1,0:T(8,128)}) async-done(((f32[256,384]{1,0:T(8,128)}, f32[256,384]{1,0:T(8,128)}), (f32[256,384]{1,0:T(8,128)}, f32[256,384]{1,0:T(8,128)})) %all-reduce.15.cloned.1.call-update) | async-done | bytes 786448
  1118.0 1.7 fusion.35
  1120.4 263.3 %all-reduce.13.cloned.1.call-done = f32[8,2048]{1,0:T(8,128)} async-done(((f32[8,2048]{1,0:T(8,128)}), f32[8,2048]{1,0:T(8,128)}) %all-reduce.13.cloned.1.call-update) | async-done | bytes 65552 | tf_op jit(solution)/shard_map/psum | solution.py:219
  1384.4 101.1 %all_gather.11 = bf16[256,128]{1,0:T(8,128)(2,1)S(1)} all-gather(bf16[8,128]{1,0:T(8,128)(2,1)S(1)} %add_convert_fusion), channel_id=1, replica_groups=mesh['req'=32,'head'=16] {'req'}, dimensions={0}, use_global_device_ids=true | all-gather | bytes 67584 | tf_op jit(solution)/shard_map/all_gather | solution.py:223
  1486.2 84.3 %all-reduce.3 = (f32[8]{0:T(128)S(1)}, f32[8]{0:T(128)S(1)}) all-reduce(f32[8]{0:T(128)S(1)} %get-tuple-element.204, f32[8]{0:T(128)S(1)} %get-tuple-element.203), channel_id=1, replica_groups=mesh['req'=32,'head'=16] {'head'}, use_global_device_ids=true, to_apply=%region_21.22 | all-reduce | flops 16 | bytes 128 | tf_op jit(solution)/shard_map/psum | solution.py:227
  (93 shorter events, 12.4 us)
Async XLA Ops:
  7.2 1110.9 %copy-start = (bf16[384,2048]{1,0:T(8,128)(2,1)S(1)}, bf16[384,2048]{1,0:T(8,128)(2,1)}, u32[]{:S(2)}) copy-start(bf16[384,2048]{1,0:T(8,128)(2,1)} %param.38) | copy-start | bytes 4718596
  7.2 113.5 %copy-start.3 = (bf16[1,256,8,128]{3,2,1,0:T(8,128)(2,1)S(1)}, bf16[1,256,8,128]{3,2,1,0:T(8,128)(2,1)}, u32[]{:S(2)}) copy-start(bf16[1,256,8,128]{3,2,1,0:T(8,128)(2,1)} %param.31) | copy-start | bytes 1572868
  67.8 54.3 %all-to-all-start = ((bf16[16,8,128]{2,1,0:T(8,128)(2,1)}), bf16[16,8,128]{2,1,0:T(8,128)(2,1)S(1)}, u32[]{:S(2)}, u32[]{:S(2)}) async-start(bf16[16,8,128]{2,1,0:T(8,128)(2,1)} %stack.3), calls=%async_computation | async-start | bytes 65536 | tf_op jit(solution)/shard_map/all_to_all | solution.py:99
  71.2 352.0 %all-reduce.9.cloned.1.call-start = ((), (), s32[]{:S(2)}) async-start(), calls=%async_computation.2 | async-start | bytes 131072 | tf_op jit(solution)/shard_map/psum | solution.py:175
  122.1 2.7 copy-start.10
  122.1 65.2 %copy-start.11 = (bf16[1,4,16,8,128]{4,3,2,1,0:T(8,128)(2,1)S(1)}, bf16[1,4,16,8,128]{4,3,2,1,0:T(8,128)(2,1)}, u32[]{:S(2)}) copy-start(bf16[1,4,16,8,128]{4,3,2,1,0:T(8,128)(2,1)} %param.34) | copy-start | bytes 393220
  122.1 301.0 %copy-start.4 = (f32[2048]{0:T(1024)S(1)}, f32[2048]{0:T(1024)}, u32[]{:S(2)}) copy-start(f32[2048]{0:T(1024)} %param.24) | copy-start | bytes 24580
  124.7 298.5 %copy-start.1 = (bf16[128,2048]{1,0:T(8,128)(2,1)S(1)}, bf16[128,2048]{1,0:T(8,128)(2,1)}, u32[]{:S(2)}) copy-start(bf16[128,2048]{1,0:T(8,128)(2,1)} %param.30) | copy-start | bytes 1572868
  124.7 298.5 %copy-start.2 = (bf16[2048,128]{1,0:T(8,128)(2,1)S(1)}, bf16[2048,128]{1,0:T(8,128)(2,1)}, u32[]{:S(2)}) copy-start(bf16[2048,128]{1,0:T(8,128)(2,1)} %param.26) | copy-start | bytes 1572868
  124.7 543.9 %copy-start.7 = (f32[2048]{0:T(1024)S(1)}, f32[2048]{0:T(1024)}, u32[]{:S(2)}) copy-start(f32[2048]{0:T(1024)} %param.35) | copy-start | bytes 24580
  125.1 560.2 %copy-start.5 = (bf16[64,384]{1,0:T(8,128)(2,1)S(1)}, bf16[64,384]{1,0:T(8,128)(2,1)}, u32[]{:S(2)}) copy-start(bf16[64,384]{1,0:T(8,128)(2,1)} %param.37) | copy-start | bytes 147460
  187.5 498.7 %copy-start.6 = (bf16[64,384]{1,0:T(8,128)(2,1)S(1)}, bf16[64,384]{1,0:T(8,128)(2,1)}, u32[]{:S(2)}) copy-start(bf16[64,384]{1,0:T(8,128)(2,1)} %param.36) | copy-start | bytes 147460
  188.2 479.4 %all-reduce.11.cloned.1.call-start = ((), (), s32[]{:S(2)}) async-start(), calls=%async_computation.3 | async-start | bytes 131072 | tf_op jit(solution)/shard_map/psum | solution.py:205
  424.9 693.1 %all-reduce.15.cloned.1.call-start = ((), (), s32[]{:S(2)}) async-start(), calls=%async_computation.5 | async-start | bytes 1572864
  686.2 799.2 %copy-start.8 = (f32[128]{0:T(128)S(1)}, f32[128]{0:T(128)}, u32[]{:S(2)}) copy-start(f32[128]{0:T(128)} %param.40) | copy-start | bytes 1540
  686.2 799.2 %copy-start.9 = (f32[128]{0:T(128)S(1)}, f32[128]{0:T(128)}, u32[]{:S(2)}) copy-start(f32[128]{0:T(128)} %param.39) | copy-start | bytes 1540
  687.2 696.4 %all-reduce.13.cloned.1.call-start = ((), (), s32[]{:S(2)}) async-start(), calls=%async_computation.4 | async-start | bytes 131072 | tf_op jit(solution)/shard_map/psum | solution.py:219
Sparse Core Ops, SparseCore 0:
  188.4 234.7 all-reduce.8
  426.3 241.2 all-reduce.10
  687.4 430.6 all-reduce.14
  1121.1 262.5 all-reduce.12
